TPU v7x, 32 devices: a whole 2x2x4 slice. The times are simulated.
32 devices in a mesh: row: 8 (over z, y), col: 4 (over x, core).
Axes of the slice: x: 2, y: 2, z: 4, core: 2. Of those that a mesh axis runs over, the one named last changes fastest.
Arguments:
- acc_feats: float32 [16384, 512], P(('row', 'col')), may hold values from -6 to 6
- content_feats: float32 [8192, 512], P('col', 'row'), may hold values from -6 to 6
- block_values: float32 [8, 4, 128, 128, 128], P('row', 'col'), may hold values from 0.02 to 1
- block_rows: int32 [8, 4, 128], P('row', 'col'), may hold values from 0 to 15, as said below
- block_cols: int32 [8, 4, 128], P('row', 'col'), may hold values from 0 to 15, as said below
- block_count: int32 [8, 4], P('row', 'col'), may hold values from 16 to 128, as said below
- w_self: float32 [512, 512], replicated, may hold values from -0.25 to 0.25
- w_neigh: float32 [512, 512], replicated, may hold values from -0.25 to 0.25
- out_grad: float32 [16384, 512], P(('row', 'col')), may hold values from -6 to 6
Outputs:
- layer_out: float32 [16384, 512], P(('row', 'col'))
- grad_acc: float32 [16384, 512], P(('row', 'col'))
- grad_content: float32 [8192, 512], P('col', 'row')
- grad_self: float32 [512, 512], replicated
- grad_neigh: float32 [512, 512], replicated
Inputs may be any that keep to these rules, and one draw needn't show every extreme that they name: `block_count`: exactly one device has 128 live slots; every other device has between 16 and 64. `block_rows`: the slots of one device hold distinct (block row, block column) positions; slots at or beyond the device's count are not part of the adjacency. `block_cols`: see block_rows.
All inputs are finite; a program needn't handle non-finite values.
Results may differ from a plain program's by a relative error of at most 0.0003.
Values sent between devices are 32-bit elements; how exact they have to be, the bound alone decides.
A program may use at most 128 MiB of HBM per device.

v0:
```python
import math

import jax
import jax.numpy as jnp
from jax import lax
from jax.sharding import PartitionSpec as P

BLK = 128
BR = 16
BC = 16


highest = lax.Precision.HIGHEST
rms_epsilon = 1e-05
slot_group = 16


def forward_tiles(block_vals, row_ids, col_ids, slot_lower, slot_upper, source):
    slot_total = block_vals.shape[0]
    group_size = min(slot_group, slot_total)
    channels = source.shape[1]
    blocks_in = source.reshape(BC, BLK, channels)
    first_turn = slot_lower // group_size
    last_turn = (slot_upper + group_size - 1) // group_size

    def forward_one_turn(turn_index, running):
        begin_slot = jnp.minimum(turn_index * group_size, slot_total - group_size)
        group_vals = lax.dynamic_slice_in_dim(block_vals, begin_slot, group_size, 0)
        group_rows = lax.dynamic_slice_in_dim(row_ids, begin_slot, group_size, 0)
        group_cols = lax.dynamic_slice_in_dim(col_ids, begin_slot, group_size, 0)
        slot_ids = begin_slot + jnp.arange(group_size, dtype=jnp.int32)
        is_live = (slot_ids >= jnp.maximum(slot_lower, turn_index * group_size)) & (
            slot_ids < slot_upper
        )
        picked = blocks_in[group_cols]
        products = jnp.einsum("kij,kjw->kiw", group_vals, picked, precision=highest)
        one_hot = (
            (group_rows[None, :] == jnp.arange(BR, dtype=jnp.int32)[:, None]) & is_live[None, :]
        ).astype(jnp.float32)
        return running + jnp.einsum("rk,kiw->riw", one_hot, products, precision=highest)

    running = lax.fori_loop(
        first_turn, last_turn, forward_one_turn, jnp.zeros((BR, BLK, channels), jnp.float32)
    )
    return running.reshape(BR * BLK, channels)


def backward_tiles(block_vals, row_ids, col_ids, slot_lower, slot_upper, grad_rows):
    slot_total = block_vals.shape[0]
    group_size = min(slot_group, slot_total)
    channels = grad_rows.shape[1]
    blocks_out = grad_rows.reshape(BR, BLK, channels)
    first_turn = slot_lower // group_size
    last_turn = (slot_upper + group_size - 1) // group_size

    def backward_one_turn(turn_index, running):
        begin_slot = jnp.minimum(turn_index * group_size, slot_total - group_size)
        group_vals = lax.dynamic_slice_in_dim(block_vals, begin_slot, group_size, 0)
        group_rows = lax.dynamic_slice_in_dim(row_ids, begin_slot, group_size, 0)
        group_cols = lax.dynamic_slice_in_dim(col_ids, begin_slot, group_size, 0)
        slot_ids = begin_slot + jnp.arange(group_size, dtype=jnp.int32)
        is_live = (slot_ids >= jnp.maximum(slot_lower, turn_index * group_size)) & (
            slot_ids < slot_upper
        )
        picked = blocks_out[group_rows]
        products = jnp.einsum("kij,kiw->kjw", group_vals, picked, precision=highest)
        one_hot = (
            (group_cols[None, :] == jnp.arange(BC, dtype=jnp.int32)[:, None]) & is_live[None, :]
        ).astype(jnp.float32)
        return running + jnp.einsum("ck,kjw->cjw", one_hot, products, precision=highest)

    running = lax.fori_loop(
        first_turn, last_turn, backward_one_turn, jnp.zeros((BC, BLK, channels), jnp.float32)
    )
    return running.reshape(BC * BLK, channels)


def tile_degree(block_vals, row_ids, live_count):
    row_sums = jnp.sum(block_vals, axis=2)
    is_live = jnp.arange(block_vals.shape[0], dtype=jnp.int32) < live_count
    one_hot = (
        (row_ids[None, :] == jnp.arange(BR, dtype=jnp.int32)[:, None]) & is_live[None, :]
    ).astype(jnp.float32)
    return jnp.dot(one_hot, row_sums, precision=highest).reshape(BR * BLK)


def local(
    acc_feats,
    content_feats,
    block_values,
    block_rows,
    block_cols,
    block_count,
    w_self,
    w_neigh,
    out_grad,
):
    own_values = block_values[0, 0]
    own_rows = block_rows[0, 0]
    own_cols = block_cols[0, 0]
    own_count = block_count[0, 0]
    degree_part = tile_degree(own_values, own_rows, own_count)
    partial_value = forward_tiles(
        own_values,
        own_rows,
        own_cols,
        0,
        own_count,
        lax.all_gather(content_feats, "row", axis=1, tiled=True),
    )
    summed, degree = (
        lax.psum_scatter(partial_value, "col", scatter_dimension=0, tiled=True),
        lax.psum_scatter(degree_part, "col", scatter_dimension=0, tiled=True),
    )
    inv_degree = lax.rsqrt(1.0 + degree)[:, None]
    neigh = summed * inv_degree
    pre_act = jnp.dot(acc_feats, w_self, precision=highest) + jnp.dot(
        neigh, w_neigh, precision=highest
    )
    sigmoid_pre = jax.nn.sigmoid(pre_act)
    activation = pre_act * sigmoid_pre
    inv_rms = lax.rsqrt(jnp.mean(activation * activation, axis=1, keepdims=True) + rms_epsilon)
    layer_out = activation * inv_rms
    d_act = (out_grad - layer_out * jnp.mean(out_grad * layer_out, axis=1, keepdims=True)) * inv_rms
    d_pre = d_act * sigmoid_pre * (1.0 + pre_act * (1.0 - sigmoid_pre))
    grad_acc = jnp.dot(d_pre, w_self.T, precision=highest)
    d_gathered = jnp.dot(d_pre, w_neigh.T, precision=highest) * inv_degree
    grad_rows = lax.all_gather(d_gathered, "col", axis=0, tiled=True)
    back_part = backward_tiles(own_values, own_rows, own_cols, 0, own_count, grad_rows)
    grad_content = lax.psum_scatter(back_part, "row", scatter_dimension=1, tiled=True)
    acc_total = acc_feats.shape[0] * lax.axis_size("row") * lax.axis_size("col")
    norm_factor = 1.0 / math.sqrt(acc_total)
    self_term = jnp.dot(acc_feats.T, d_pre, precision=highest)
    neigh_term = jnp.dot(neigh.T, d_pre, precision=highest)
    grad_self, grad_neigh = lax.psum((self_term, neigh_term), ("row", "col"))
    return (layer_out, grad_acc, grad_content, grad_self * norm_factor, grad_neigh * norm_factor)


def solution(mesh):
    in_specs = (
        P(("row", "col"), None),
        P("col", "row"),
        P("row", "col", None, None, None),
        P("row", "col", None),
        P("row", "col", None),
        P("row", "col"),
        P(),
        P(),
        P(("row", "col"), None),
    )
    out_specs = (P(("row", "col"), None), P(("row", "col"), None), P("col", "row"), P(), P())
    return jax.shard_map(local, mesh=mesh, in_specs=in_specs, out_specs=out_specs, check_vma=False)
```

profile of v0, /device:TPU:0, one launch (start us, length us, event | category | flops | bytes accessed | tf_op | source)
XLA Modules:
  0.0 639.2 jit_solution(16231107461652841880)
XLA Ops:
  7.2 0.7 all-gather.3.cloned.1.call-update
  8.6 77.6 %all-gather.3.cloned.1.call-done = f32[2048,512]{0,1:T(8,128)} async-done(((f32[2048,64]{0,1:T(8,128)}), f32[2048,512]{0,1:T(8,128)}) %all-gather.3.cloned.1.call-update) | async-done | bytes 4194320 | tf_op jit(solution)/shard_map/all_gather | solution.py:109
  86.3 5.4 copy.23
  91.6 2.5 broadcast.73.clone
  94.1 79.9 %while.20 = (s32[]{:T(128)}, f32[16,128,512]{2,0,1:T(8,128)}, s32[]{:T(128)}, s32[128]{0:T(128)S(1)}, s32[]{:T(128)}, /*index=5*/f32[128,128,128]{2,1,0:T(8,128)...) while((s32[]{:T(128)}, f32[16,128,512]{2,0,1:T(8,128)}, ...), condition=%wide.region_1.2_spmd, body=%wide.region_0.0_spmd.sunk | while | flops 1812989440 | bytes 63967984 | solution.py:42
  94.1 0.7 compare_and_fusion.4
  95.0 5.0 gather_fusion
  99.9 6.0 fusion.68
  106.0 6.1 fusion.69
  112.1 2.0 copy-done.5
  114.1 0.7 compare_and_fusion.4
  114.9 5.0 gather_fusion
  119.8 6.0 fusion.68
  125.9 6.1 fusion.69
  132.0 2.0 copy-done.5
  134.8 5.0 gather_fusion
  139.8 6.0 fusion.68
  145.8 6.1 fusion.69
  151.9 2.0 copy-done.5
  154.7 5.0 gather_fusion
  159.7 6.0 fusion.68
  165.7 6.1 fusion.69
  171.8 2.0 copy-done.5
  174.0 6.6 %copy.24 = f32[16,128,512]{2,1,0:T(8,128)} copy(f32[16,128,512]{2,0,1:T(8,128)} %get-tuple-element.91) | data formatting | bytes 8388608 | tf_op jit(solution)/shard_map/while | solution.py:42
  180.7 5.7 reduce_sum.27
  186.4 1.6 copy.26
  189.4 5.8 all-reduce
  195.2 4.1 fusion.37
  199.3 102.1 %reduce-scatter.3.cloned.1.call-done = f32[512,512]{1,0:T(8,128)} async-done(((f32[2048,512]{1,0:T(8,128)}), f32[512,512]{1,0:T(8,128)}) %reduce-scatter.3.cloned.1.call-update) | async-done | bytes 1048592 | tf_op jit(solution)/shard_map/reduce_scatter | solution.py:112
  301.4 3.9 multiply_reduce_fusion.1
  305.7 1.5 add_multiply_fusion
  307.2 4.4 convolution_multiply_fusion
  311.6 9.6 %all-reduce.4.cloned.1.call-start = ((), (), s32[]{:S(2)}) async-start(), calls=%async_computation.6 | async-start | bytes 4194304 | tf_op jit(solution)/shard_map/psum | solution.py:135
  321.3 2.9 convolution_bitcast_fusion
  324.2 4.2 fusion.27
  328.5 17.8 %all-gather.5.cloned.1.call-done = f32[2048,512]{1,0:T(8,128)} async-done(((f32[512,512]{1,0:T(8,128)}), f32[2048,512]{1,0:T(8,128)}) %all-gather.5.cloned.1.call-update) | async-done | bytes 4194320 | tf_op jit(solution)/shard_map/all_gather | solution.py:128
  346.2 2.5 broadcast.73
  348.7 92.5 %while.21 = (s32[]{:T(128)}, f32[16,128,512]{2,0,1:T(8,128)}, s32[]{:T(128)}, s32[128]{0:T(128)S(1)}, s32[]{:T(128)}, /*index=5*/f32[128,128,128]{2,1,0:T(8,128)...) while((s32[]{:T(128)}, f32[16,128,512]{2,0,1:T(8,128)}, ...), condition=%wide.region_8.9_spmd, body=%wide.region_7.8_spmd.sunk | while | flops 1812989440 | bytes 63967984 | solution.py:72
  349.6 5.0 gather_fusion.1
  354.5 9.1 %fusion.74 = f32[16,128,512]{2,1,0:T(8,128)S(1)} fusion(f32[16,128,512]{2,1,0:T(8,128)} %gather_fusion.1, f32[128,128,128]{2,1,0:T(8,128)} %get-tuple-element.313, s32[]{:T(128)S(6)} %select_n.32), kind=kOutput, calls=%fused_computation.19.clone.1 | convolution fusion | flops 1610612736 | bytes 9437188 | tf_op jit(solution)/shard_map/while/body/kij,kiw->kjw/dot_general | solution.py:66
  363.7 6.1 fusion.75
  369.8 2.0 copy-done.3
  372.6 5.0 gather_fusion.1
  377.6 9.2 %fusion.74 = f32[16,128,512]{2,1,0:T(8,128)S(1)} fusion(f32[16,128,512]{2,1,0:T(8,128)} %gather_fusion.1, f32[128,128,128]{2,1,0:T(8,128)} %get-tuple-element.313, s32[]{:T(128)S(6)} %select_n.32), kind=kOutput, calls=%fused_computation.19.clone.1 | convolution fusion | flops 1610612736 | bytes 9437188 | tf_op jit(solution)/shard_map/while/body/kij,kiw->kjw/dot_general | solution.py:66
  386.8 6.1 fusion.75
  392.9 2.0 copy-done.3
  395.7 5.0 gather_fusion.1
  400.7 9.1 %fusion.74 = f32[16,128,512]{2,1,0:T(8,128)S(1)} fusion(f32[16,128,512]{2,1,0:T(8,128)} %gather_fusion.1, f32[128,128,128]{2,1,0:T(8,128)} %get-tuple-element.313, s32[]{:T(128)S(6)} %select_n.32), kind=kOutput, calls=%fused_computation.19.clone.1 | convolution fusion | flops 1610612736 | bytes 9437188 | tf_op jit(solution)/shard_map/while/body/kij,kiw->kjw/dot_general | solution.py:66
  409.9 6.1 fusion.75
  416.0 2.0 copy-done.3
  418.8 5.0 gather_fusion.1
  423.7 9.1 %fusion.74 = f32[16,128,512]{2,1,0:T(8,128)S(1)} fusion(f32[16,128,512]{2,1,0:T(8,128)} %gather_fusion.1, f32[128,128,128]{2,1,0:T(8,128)} %get-tuple-element.313, s32[]{:T(128)S(6)} %select_n.32), kind=kOutput, calls=%fused_computation.19.clone.1 | convolution fusion | flops 1610612736 | bytes 9437188 | tf_op jit(solution)/shard_map/while/body/kij,kiw->kjw/dot_general | solution.py:66
  432.9 6.1 fusion.75
  439.1 2.0 copy-done.3
  441.2 5.9 copy.27
  447.1 6.1 copy.45
  453.3 1.2 copy-done.9
  454.5 1.3 copy.29
  455.8 4.4 fusion.38
  460.2 26.4 %all-reduce.4.cloned.1.call-done = (f32[512,512]{0,1:T(8,128)}, f32[512,512]{0,1:T(8,128)}) async-done(((f32[512,512]{0,1:T(8,128)}, f32[512,512]{0,1:T(8,128)}), (f32[512,512]{0,1:T(8,128)}, f32[512,512]{0,1:T(8,128)})) %all-reduce.4.cloned.1.call-update) | async-done | bytes 2097168 | tf_op jit(solution)/shard_map/psum | solution.py:135
  486.6 1.9 broadcast_multiply_fusion
  488.5 1.3 copy.31
  489.9 1.3 copy.30
  491.2 141.3 %reduce-scatter.5.cloned.1.call-done = f32[2048,64]{0,1:T(8,128)} async-done(((f32[2048,512]{0,1:T(8,128)}), f32[2048,64]{0,1:T(8,128)}) %reduce-scatter.5.cloned.1.call-update) | async-done | bytes 524304 | tf_op jit(solution)/shard_map/reduce_scatter | solution.py:130
  (86 shorter events, 6.7 us)
Async XLA Ops:
  7.2 294.2 %copy-start = (f32[512,512]{1,0:T(8,128)S(1)}, f32[512,512]{1,0:T(8,128)}, u32[]{:S(2)}) copy-start(f32[512,512]{1,0:T(8,128)} %param.20) | copy-start | bytes 3145732
  7.2 79.1 %all-gather.3.cloned.1.call-start = ((), (), s32[]{:S(2)}) async-start(), calls=%async_computation.2 | async-start | bytes 4718592 | tf_op jit(solution)/shard_map/all_gather | solution.py:109
  7.9 293.5 %reduce-scatter.3.cloned.1.call-start = ((), (), s32[]{:S(2)}) async-start(), calls=%async_computation.3 | async-start | bytes 5242880 | tf_op jit(solution)/shard_map/reduce_scatter | solution.py:112
  91.6 2.5 copy-start.10
  91.6 2.5 copy-start.11
  99.9 6.0 copy-start.4
  112.1 2.0 copy-start.5
  119.8 6.0 copy-start.4
  132.0 2.0 copy-start.5
  139.8 6.0 copy-start.4
  151.9 2.0 copy-start.5
  159.7 6.0 copy-start.4
  171.8 2.0 copy-start.5
  180.6 165.6 %all-gather.5.cloned.1.call-start = ((), (), s32[]{:S(2)}) async-start(), calls=%async_computation.4 | async-start | bytes 5242880 | tf_op jit(solution)/shard_map/all_gather | solution.py:128
  180.7 7.3 %copy-start.12 = (u32[32]{0:T(128)S(1)}, u32[32]{0:T(128)}, u32[]{:S(2)}) copy-start(u32[32]{0:T(128)} %constant.66) | copy-start | bytes 388
  180.7 14.5 %copy-start.6 = (f32[512,512]{1,0:T(8,128)S(1)}, f32[512,512]{1,0:T(8,128)}, u32[]{:S(2)}) copy-start(f32[512,512]{1,0:T(8,128)} %param.13) | copy-start | bytes 3145732
  307.2 14.1 %copy-start.7 = (f32[512,512]{1,0:T(8,128)S(1)}, f32[512,512]{1,0:T(8,128)}, u32[]{:S(2)}) copy-start(f32[512,512]{1,0:T(8,128)} %param.13) | copy-start | bytes 3145732
  311.6 175.0 %all-reduce.4.cloned.1.call-start = ((), (), s32[]{:S(2)}) async-start(), calls=%async_computation.6 | async-start | bytes 4194304 | tf_op jit(solution)/shard_map/psum | solution.py:135
  328.4 304.0 %reduce-scatter.5.cloned.1.call-start = ((), (), s32[]{:S(2)}) async-start(), calls=%async_computation.5 | async-start | bytes 4718592 | tf_op jit(solution)/shard_map/reduce_scatter | solution.py:130
  354.5 9.1 %copy-start.2 = (f32[16,128,512]{2,0,1:T(8,128)S(1)}, f32[16,128,512]{2,0,1:T(8,128)}, u32[]{:S(2)}) copy-start(f32[16,128,512]{2,0,1:T(8,128)} %get-tuple-element.296) | copy-start | bytes 12582916 | tf_op jit(solution)/shard_map/while
  369.8 2.0 copy-start.3
  377.6 9.2 %copy-start.2 = (f32[16,128,512]{2,0,1:T(8,128)S(1)}, f32[16,128,512]{2,0,1:T(8,128)}, u32[]{:S(2)}) copy-start(f32[16,128,512]{2,0,1:T(8,128)} %get-tuple-element.296) | copy-start | bytes 12582916 | tf_op jit(solution)/shard_map/while
  392.9 2.0 copy-start.3
  400.7 9.1 %copy-start.2 = (f32[16,128,512]{2,0,1:T(8,128)S(1)}, f32[16,128,512]{2,0,1:T(8,128)}, u32[]{:S(2)}) copy-start(f32[16,128,512]{2,0,1:T(8,128)} %get-tuple-element.296) | copy-start | bytes 12582916 | tf_op jit(solution)/shard_map/while
  416.0 2.0 copy-start.3
  423.7 9.2 %copy-start.2 = (f32[16,128,512]{2,0,1:T(8,128)S(1)}, f32[16,128,512]{2,0,1:T(8,128)}, u32[]{:S(2)}) copy-start(f32[16,128,512]{2,0,1:T(8,128)} %get-tuple-element.296) | copy-start | bytes 12582916 | tf_op jit(solution)/shard_map/while
  439.0 2.0 copy-start.3
  453.2 1.2 copy-start.9
  453.2 2.5 copy-start.8
  486.6 145.8 %copy-start.1 = (f32[512,512]{1,0:T(8,128)S(1)}, f32[512,512]{1,0:T(8,128)}, u32[]{:S(2)}) copy-start(f32[512,512]{1,0:T(8,128)} %param.20) | copy-start | bytes 3145732
Sparse Core Ops, SparseCore 0:
  10.1 76.0 all-gather.2
  180.8 120.5 reduce-scatter.2
  311.7 34.4 all-gather.4
  352.5 134.0 all-reduce.3
  490.7 141.7 reduce-scatter.4
where the time goes:
time: 648 us; the launch traced here: 639 us
  waiting for transfers between devices  366 us (56%)
  matrix products  134 us (21%)
  local copies, waits for them, and re-layouts  92.4 us (14%)
  other arithmetic  15.5 us (2%)
  between operations  15.5 us (2%)
  starting transfers between devices  9.78 us (2%)
    reduce_scatter x1, waiting for transfers between devices, local(): lax.psum_scatter(back_part, 'row', scatter_dimension=1, tiled=True)  141 us
    reduce_scatter x1, waiting for transfers between devices, local(): lax.psum_scatter(partial_value, 'col', scatter_dimension=0, tiled=True)  102 us
    all_gather x1, waiting for transfers between devices, local(): lax.all_gather(content_feats, 'row', axis=1, tiled=True)  77.6 us
    dot_general x4, matrix products, backward_one_turn(): products = jnp.einsum('kij,kiw->kjw', group_vals, picked, precision=highest)  36.6 us
    psum x1, waiting for transfers between devices, local(): grad_self, grad_neigh = lax.psum((self_term, neigh_term), ('row', 'col'))  26.4 us
    dot_general x4, matrix products, backward_one_turn(): jnp.einsum('ck,kjw->cjw', one_hot, products, precision=highest)  24.5 us
    dot_general x4, matrix products, forward_one_turn(): jnp.einsum('rk,kiw->riw', one_hot, products, precision=highest)  24.5 us
    dot_general x4, matrix products, forward_one_turn(): products = jnp.einsum('kij,kjw->kiw', group_vals, picked, precision=highest)  24 us
  transfers between devices with their start and end apart: 5, of which 5 were waited for; matrix products, arithmetic and copies ran while one was open for 20% of the time, Pallas kernels for 0%

commit v1 on v0

v1 whole, which is shorter than its diff:
```python
import functools
import math

import jax
import jax.numpy as jnp
from jax import lax
from jax.experimental import pallas as pl
from jax.experimental.pallas import tpu as pltpu
from jax.sharding import PartitionSpec as P

BLK = 128
BR = 16
BC = 16
GROUP = 8
PAD = 8
VMEM_LIMIT = 48 * 1024 * 1024
high = lax.Precision.HIGH
rms_epsilon = 1e-05


def split(x):
    hi = x.astype(jnp.bfloat16)
    lo = (x - hi.astype(jnp.float32)).astype(jnp.bfloat16)
    return hi, lo


def forward_kernel(per_chunk, rows_ref, cols_ref, count_ref, vals_ref, source_ref, out_ref, xs, degs):
    step = pl.program_id(0)
    chunks, chunk_rows, _ = out_ref.shape

    @pl.when(step == 0)
    def _():
        for block in range(BC):
            hi, lo = split(source_ref[:, block * BLK : (block + 1) * BLK].T)
            xs[block, 0:BLK, :] = hi
            xs[block, BLK:, :] = lo
        out_ref[...] = jnp.zeros_like(out_ref)
        degs[...] = jnp.zeros_like(degs)

    ones = jnp.ones((8, 2 * BLK), jnp.bfloat16)
    for k in range(GROUP):
        slot = step * GROUP + k

        @pl.when(slot < count_ref[0])
        def _():
            row, col = rows_ref[slot], cols_ref[slot]
            hi, lo = split(vals_ref[k])
            left = jnp.concatenate(
                [jnp.concatenate([hi, hi], axis=1), jnp.concatenate([lo, lo], axis=1)], axis=0
            )
            product = jnp.dot(left, xs[col], preferred_element_type=jnp.float32)
            chunk = row // per_chunk
            begin = pl.multiple_of((row - chunk * per_chunk) * BLK, BLK)
            out_ref[chunk, pl.ds(begin, BLK), :] += product[:BLK] + product[BLK:]
            degs[row] += lax.dot_general(
                ones,
                jnp.concatenate([hi, lo], axis=1),
                (((1,), (1,)), ((), ())),
                preferred_element_type=jnp.float32,
            )

    @pl.when(step == pl.num_programs(0) - 1)
    def _():
        for row in range(BR):
            chunk, place = row // per_chunk, row % per_chunk
            out_ref[chunk, chunk_rows - PAD :, place * BLK : (place + 1) * BLK] = degs[row]


def backward_kernel(rows_ref, cols_ref, count_ref, vals_ref, grad_ref, out_ref, gs):
    step = pl.program_id(0)

    @pl.when(step == 0)
    def _():
        for block in range(BR):
            hi, lo = split(grad_ref[block * BLK : (block + 1) * BLK, :].T)
            gs[block, :, 0:BLK] = hi
            gs[block, :, BLK:] = lo
        out_ref[...] = jnp.zeros_like(out_ref)

    for k in range(GROUP):
        slot = step * GROUP + k

        @pl.when(slot < count_ref[0])
        def _():
            row, col = rows_ref[slot], cols_ref[slot]
            hi, lo = split(vals_ref[k])
            both = jnp.concatenate([hi, lo], axis=1)
            right = jnp.concatenate([both, both], axis=0)
            product = jnp.dot(gs[row], right, preferred_element_type=jnp.float32)
            begin = pl.multiple_of(col * BLK, BLK)
            out_ref[:, pl.ds(begin, BLK)] += product[:, :BLK] + product[:, BLK:]


def values_index(step, rows_ref, cols_ref, count_ref):
    return (jnp.minimum(step, (count_ref[0] - 1) // GROUP), 0, 0)


def whole(*shape):
    return pl.BlockSpec(shape, lambda step, *_: (0,) * len(shape))


def forward_tiles(vals, rows, cols, count, source, chunks):
    channels = source.shape[0]
    per_chunk = BR // chunks
    chunk_rows = per_chunk * BLK + PAD
    slots = vals.shape[0]
    return pl.pallas_call(
        functools.partial(forward_kernel, per_chunk),
        out_shape=jax.ShapeDtypeStruct((chunks, chunk_rows, channels), jnp.float32),
        grid_spec=pltpu.PrefetchScalarGridSpec(
            num_scalar_prefetch=3,
            grid=(slots // GROUP,),
            in_specs=[
                pl.BlockSpec((GROUP, BLK, BLK), values_index),
                whole(channels, BC * BLK),
            ],
            out_specs=whole(chunks, chunk_rows, channels),
            scratch_shapes=[
                pltpu.VMEM((BC, 2 * BLK, channels), jnp.bfloat16),
                pltpu.VMEM((BR, 8, BLK), jnp.float32),
            ],
        ),
        compiler_params=pltpu.CompilerParams(vmem_limit_bytes=VMEM_LIMIT),
        cost_estimate=pl.CostEstimate(
            flops=slots * BLK * BLK * channels * 4, bytes_accessed=16_000_000, transcendentals=0
        ),
    )(rows, cols, count, vals, source)


def backward_tiles(vals, rows, cols, count, grad_rows):
    channels = grad_rows.shape[1]
    slots = vals.shape[0]
    return pl.pallas_call(
        backward_kernel,
        out_shape=jax.ShapeDtypeStruct((channels, BC * BLK), jnp.float32),
        grid_spec=pltpu.PrefetchScalarGridSpec(
            num_scalar_prefetch=3,
            grid=(slots // GROUP,),
            in_specs=[
                pl.BlockSpec((GROUP, BLK, BLK), values_index),
                whole(BR * BLK, channels),
            ],
            out_specs=whole(channels, BC * BLK),
            scratch_shapes=[pltpu.VMEM((BR, channels, 2 * BLK), jnp.bfloat16)],
        ),
        compiler_params=pltpu.CompilerParams(vmem_limit_bytes=VMEM_LIMIT),
        cost_estimate=pl.CostEstimate(
            flops=slots * BLK * BLK * channels * 4, bytes_accessed=16_000_000, transcendentals=0
        ),
    )(rows, cols, count, vals, grad_rows)


def local(
    acc_feats,
    content_feats,
    block_values,
    block_rows,
    block_cols,
    block_count,
    w_self,
    w_neigh,
    out_grad,
):
    vals = block_values[0, 0]
    rows = block_rows[0, 0]
    cols = block_cols[0, 0]
    count = block_count[0]
    accounts = acc_feats.shape[0]
    chunks = lax.axis_size("col")

    source = lax.all_gather(content_feats.T, "row", axis=0, tiled=True)
    partial = forward_tiles(vals, rows, cols, count, source, chunks)
    summed = lax.psum_scatter(partial, "col", scatter_dimension=0, tiled=True)[0]
    degree = summed[accounts].reshape(-1)[:accounts]
    inv_degree = lax.rsqrt(1.0 + degree)[:, None]
    neigh = summed[:accounts] * inv_degree
    pre_act = jnp.dot(acc_feats, w_self, precision=high) + jnp.dot(neigh, w_neigh, precision=high)
    sigmoid_pre = jax.nn.sigmoid(pre_act)
    activation = pre_act * sigmoid_pre
    inv_rms = lax.rsqrt(jnp.mean(activation * activation, axis=1, keepdims=True) + rms_epsilon)
    layer_out = activation * inv_rms
    d_act = (out_grad - layer_out * jnp.mean(out_grad * layer_out, axis=1, keepdims=True)) * inv_rms
    d_pre = d_act * sigmoid_pre * (1.0 + pre_act * (1.0 - sigmoid_pre))
    d_gathered = jnp.dot(d_pre, w_neigh.T, precision=high) * inv_degree
    grad_rows = lax.all_gather(d_gathered, "col", axis=0, tiled=True)
    back_part = backward_tiles(vals, rows, cols, count, grad_rows)
    grad_content = lax.psum_scatter(back_part, "row", scatter_dimension=0, tiled=True).T
    grad_acc = jnp.dot(d_pre, w_self.T, precision=high)
    acc_total = accounts * lax.axis_size("row") * lax.axis_size("col")
    norm_factor = 1.0 / math.sqrt(acc_total)
    both = jnp.concatenate([acc_feats, neigh], axis=1)
    weight_term = lax.dot_general(both, d_pre, (((0,), (0,)), ((), ())), precision=high)
    weight_grads = lax.psum(weight_term * norm_factor, ("row", "col"))
    features = acc_feats.shape[1]
    return (layer_out, grad_acc, grad_content, weight_grads[:features], weight_grads[features:])


def solution(mesh):
    in_specs = (
        P(("row", "col"), None),
        P("col", "row"),
        P("row", "col", None, None, None),
        P("row", "col", None),
        P("row", "col", None),
        P("row", "col"),
        P(),
        P(),
        P(("row", "col"), None),
    )
    out_specs = (P(("row", "col"), None), P(("row", "col"), None), P("col", "row"), P(), P())
    return jax.shard_map(local, mesh=mesh, in_specs=in_specs, out_specs=out_specs, check_vma=False)
```

time: 648 us -> 447 us (0.69); the launches traced: 639 us -> 446 us
  matrix products: 134 us -> 16.1 us
  local copies, waits for them, and re-layouts: 92.4 us -> 12.8 us
  Pallas kernels: 0 us -> 21.5 us
  other arithmetic: 15.5 us -> 4 us
  waiting for transfers between devices: 366 us -> 377 us
  starting transfers between devices: 9.78 us -> 0.38 us
    dot_general x23 -> x5, matrix products: 134 us -> 16.1 us  [the longest x1 6 us: local(): lax.dot_general(both, d_pre, (((0,), (0,)), ((), ())), precision=high)]
    psum x1, waiting for transfers between devices: 26.4 us -> 122 us  [local(): weight_grads = lax.psum(weight_term * norm_factor, ('row', 'col'))]
    reduce_scatter x2, waiting for transfers between devices: 243 us -> 148 us  [the longest x1 88 us: local(): lax.psum_scatter(back_part, 'row', scatter_dimension=0, tiled=True)]
    gather x8 -> x0, local copies, waits for them, and re-layouts: 39.8 us -> none  [the longest x4 20 us: backward_one_turn(): picked = blocks_out[group_rows]]
    while x34 -> x0, local copies, waits for them, and re-layouts: 28.2 us -> none
    pallas_call x0 -> x2, Pallas kernels: none -> 21.5 us  [the longest x1 11.1 us: forward_tiles(): pl.pallas_call(functools.partial(forward_kernel, per_chunk), out_shape=ja...]
    all_gather x1, waiting for transfers between devices: 17.8 us -> 28.3 us  [local(): grad_rows = lax.all_gather(d_gathered, 'col', axis=0, tiled=True)]
    psum x1, starting transfers between devices: 9.62 us -> 0.04 us  [local(): weight_grads = lax.psum(weight_term * norm_factor, ('row', 'col'))]
  transfers between devices with their start and end apart: 5 -> 5, of which waited for: 5 -> 5; matrix products, arithmetic and copies ran while one was open for 20% -> 4% of each run, Pallas kernels for 0% -> 2%
where the time goes in v1:
time: 447 us; the launch traced here: 446 us
  waiting for transfers between devices  377 us (84%)
  Pallas kernels  21.5 us (5%)
  matrix products  16.1 us (4%)
  between operations  14.5 us (3%)
  local copies, waits for them, and re-layouts  12.8 us (3%)
    psum x1, waiting for transfers between devices, local(): weight_grads = lax.psum(weight_term * norm_factor, ('row', 'col'))  122 us
    reduce_scatter x1, waiting for transfers between devices, local(): lax.psum_scatter(back_part, 'row', scatter_dimension=0, tiled=True)  88 us
    all_gather x1, waiting for transfers between devices, local(): source = lax.all_gather(content_feats.T, 'row', axis=0, tiled=True)  77.7 us
    reduce_scatter x1, waiting for transfers between devices, local(): lax.psum_scatter(partial, 'col', scatter_dimension=0, tiled=True)[0]  59.8 us
    all_gather x1, waiting for transfers between devices, local(): grad_rows = lax.all_gather(d_gathered, 'col', axis=0, tiled=True)  28.3 us
    pallas_call x1, Pallas kernels, forward_tiles(): pl.pallas_call(functools.partial(forward_kernel, per_chunk), out_shape=ja...  11.1 us
    pallas_call x1, Pallas kernels, backward_tiles(): pl.pallas_call(backward_kernel, out_shape=jax.ShapeDtypeStruct((channels,...  10.4 us
    unnamed x26, local copies, waits for them, and re-layouts  9.74 us
  transfers between devices with their start and end apart: 5, of which 5 were waited for; matrix products, arithmetic and copies ran while one was open for 4% of the time, Pallas kernels for 2%

profile of v1, /device:TPU:0, one launch (start us, length us, event | category | flops | bytes accessed | tf_op | source)
XLA Modules:
  0.0 445.9 jit_solution(11223199957157668275)
XLA Ops:
  7.2 0.0 copy-start
  7.2 0.0 all-gather.3.cloned.1.call-start
  7.2 0.7 all-gather.3.cloned.1.call-update
  7.9 0.0 reduce-scatter.3.cloned.1.call-start
  8.6 77.7 %all-gather.3.cloned.1.call-done.source_ref = f32[512,2048]{1,0:T(8,128)} async-done(((f32[64,2048]{1,0:T(8,128)}), f32[512,2048]{1,0:T(8,128)}) %all-gather.3.cloned.1.call-update) | async-done | bytes 4194320 | tf_op jit(solution)/shard_map/all_gather | solution.py:171
  86.3 0.0 copy-start.2
  86.3 2.2 copy-done.2
  88.5 0.0 copy-start.3
  88.5 0.7 copy-done.3
  89.1 0.0 copy-start.5
  89.1 0.7 copy-done.5
  89.8 11.1 %shard_map.128 = f32[4,520,512]{2,1,0:T(8,128)} custom-call(s32[128]{0:T(128)S(1)} %bitcast.22, s32[128]{0:T(128)S(1)} %bitcast.24, s32[1]{0:T(128)} %bitcast.20.count_ref, f32[128,128,128]{2,1,0:T(8,128)} %bitcast.26, f32[512,2048]{1,0:T(8,128)S(1)} %copy-done.2), custom_call_target="tpu_custom_call" | custom-call | flops 4294967296 | bytes 16000000 | tf_op jit(solution)/shard_map/pallas_call | solution.py:107
  100.9 0.0 reduce-scatter.3.cloned.1.call-update
  100.9 0.0 copy-start.7
  100.9 0.0 all-gather.5.cloned.1.call-start
  101.0 1.6 copy.15
  102.6 0.0 copy-done.7
  102.6 3.2 fusion.12
  105.8 0.0 copy-start.11
  105.8 59.8 %reduce-scatter.3.cloned.1.call-done = f32[1,520,512]{2,1,0:T(8,128)} async-done(((f32[4,520,512]{2,1,0:T(8,128)}), f32[1,520,512]{2,1,0:T(8,128)}) %reduce-scatter.3.cloned.1.call-update) | async-done | bytes 1064976 | tf_op jit(solution)/shard_map/reduce_scatter | solution.py:173
  165.6 0.7 fusion.9
  166.3 1.4 fusion.7
  167.7 0.0 copy-done
  167.7 0.0 copy-done.11
  167.7 0.0 copy-start.10
  167.7 1.2 multiply_reduce_fusion.1
  169.0 0.0 copy-done.10
  169.0 0.4 multiply_reduce_fusion
  169.4 1.5 add_multiply_fusion
  170.9 0.0 copy-start.8
  170.9 2.8 convolution_multiply_fusion
  173.7 0.0 all-gather.5.cloned.1.call-update
  173.7 0.0 all-reduce.2.cloned.1.call-start
  173.8 0.0 copy-done.8
  173.8 6.0 %fusion.4 = f32[1024,512]{1,0:T(8,128)} fusion(f32[512,512]{0,1:T(8,128)S(1)} %get-tuple-element.12, f32[512,512]{1,0:T(8,128)} %copy-done.10, f32[512,512]{1,0:T(8,128)S(1)} %copy-done.8), kind=kOutput, calls=%fused_computation.4 | convolution fusion | flops 1611661312 | bytes 5242880 | tf_op jit(solution)/shard_map/dot_general | solution.py:192
  179.8 0.0 copy-start.4
  179.8 0.0 copy-start.6
  179.8 0.0 all-reduce.2.cloned.1.call-update
  179.8 0.2 reduce-scatter.5.cloned.1.call-start
  180.1 28.3 %all-gather.5.cloned.1.call-done.grad_ref = f32[2048,512]{1,0:T(8,128)} async-done(((f32[512,512]{1,0:T(8,128)}), f32[2048,512]{1,0:T(8,128)}) %all-gather.5.cloned.1.call-update) | async-done | bytes 4194320 | tf_op jit(solution)/shard_map/all_gather | solution.py:185
  208.4 0.0 copy-done.4
  208.4 0.0 copy-done.6
  208.4 10.4 %shard_map.129 = f32[512,2048]{1,0:T(8,128)S(1)} custom-call(s32[128]{0:T(128)S(1)} %bitcast.23, s32[128]{0:T(128)S(1)} %bitcast.25, s32[1]{0:T(128)} %bitcast.21.count_ref, f32[128,128,128]{2,1,0:T(8,128)} %bitcast.27, f32[2048,512]{1,0:T(8,128)} %all-gather.5.cloned.1.call-done.grad_ref), custom_call_target="tpu_custom_call" | custom-call | flops 4294967296 | bytes 16000000 | tf_op jit(solution)/shard_map/pallas_call | solution.py:133
  218.8 0.0 copy-start.1
  218.8 1.9 copy-done.1
  220.7 0.0 reduce-scatter.5.cloned.1.call-update
  220.8 0.0 copy-start.9
  220.8 2.6 copy.16
  223.4 0.0 copy-done.9
  223.4 2.8 fusion.13
  226.2 122.1 %all-reduce.2.cloned.1.call-done = f32[1024,512]{1,0:T(8,128)} async-done(((f32[1024,512]{1,0:T(8,128)}), f32[1024,512]{1,0:T(8,128)}) %all-reduce.2.cloned.1.call-update) | async-done | bytes 2097168 | tf_op jit(solution)/shard_map/psum | solution.py:193
  348.3 3.0 fusion.11
  351.3 88.0 %reduce-scatter.5.cloned.1.call-done = f32[64,2048]{1,0:T(8,128)} async-done(((f32[512,2048]{1,0:T(8,128)}), f32[64,2048]{1,0:T(8,128)}) %reduce-scatter.5.cloned.1.call-update) | async-done | bytes 524304 | tf_op jit(solution)/shard_map/reduce_scatter | solution.py:187
  (2 shorter events, 0.0 us)
Async XLA Ops:
  7.2 160.5 %copy-start = (f32[512,512]{1,0:T(8,128)S(1)}, f32[512,512]{1,0:T(8,128)}, u32[]{:S(2)}) copy-start(f32[512,512]{1,0:T(8,128)} %param.16) | copy-start | bytes 3145732
  7.2 79.1 %all-gather.3.cloned.1.call-start = ((), (), s32[]{:S(2)}) async-start(), calls=%async_computation.2 | async-start | bytes 4718592 | tf_op jit(solution)/shard_map/all_gather | solution.py:171
  7.9 157.7 %reduce-scatter.3.cloned.1.call-start = ((), (), s32[]{:S(2)}) async-start(), calls=%async_computation.3 | async-start | bytes 5324800 | tf_op jit(solution)/shard_map/reduce_scatter | solution.py:173
  86.3 2.2 copy-start.2
  88.5 0.7 copy-start.3
  89.1 0.7 copy-start.5
  100.9 1.7 copy-start.7
  100.9 107.5 %all-gather.5.cloned.1.call-start = ((), (), s32[]{:S(2)}) async-start(), calls=%async_computation.4 | async-start | bytes 5242880 | tf_op jit(solution)/shard_map/all_gather | solution.py:185
  105.8 61.9 %copy-start.11 = (f32[512,512]{0,1:T(8,128)S(1)}, f32[512,512]{0,1:T(8,128)}, u32[]{:S(2)}) copy-start(f32[512,512]{0,1:T(8,128)} %fusion.12) | copy-start | bytes 3145732
  167.7 1.3 copy-start.10
  170.9 2.9 copy-start.8
  173.7 174.6 %all-reduce.2.cloned.1.call-start = ((), (), s32[]{:S(2)}) async-start(), calls=%async_computation.6 | async-start | bytes 4194304 | tf_op jit(solution)/shard_map/psum | solution.py:193
  179.8 28.6 %copy-start.4 = (s32[1,1,128]{2,1,0:T(1,128)S(1)}, s32[1,1,128]{2,1,0:T(1,128)}, u32[]{:S(2)}) copy-start(s32[1,1,128]{2,1,0:T(1,128)} %param.12) | copy-start | bytes 1540
  179.8 28.6 %copy-start.6 = (s32[1,1,128]{2,1,0:T(1,128)S(1)}, s32[1,1,128]{2,1,0:T(1,128)}, u32[]{:S(2)}) copy-start(s32[1,1,128]{2,1,0:T(1,128)} %param.13) | copy-start | bytes 1540
  179.8 259.5 %reduce-scatter.5.cloned.1.call-start = ((), (), s32[]{:S(2)}) async-start(), calls=%async_computation.5 | async-start | bytes 4718592 | tf_op jit(solution)/shard_map/reduce_scatter | solution.py:187
  218.8 2.0 copy-start.1
  220.8 2.6 copy-start.9
Sparse Core Ops, SparseCore 0:
  10.1 76.0 all-gather.2
  101.0 64.5 reduce-scatter.2
  173.9 34.4 all-gather.4
  214.4 133.8 all-reduce.1
  352.4 86.9 reduce-scatter.4

commit v2 on v1

--- a/solution.py
+++ b/solution.py
@@ -89,6 +89,157 @@
             product = jnp.dot(gs[row], right, preferred_element_type=jnp.float32)
             begin = pl.multiple_of(col * BLK, BLK)
             out_ref[:, pl.ds(begin, BLK)] += product[:, :BLK] + product[:, BLK:]
+
+
+MESH = pl.DeviceIdType.MESH
+
+
+def place_of(index, size):
+    upper, lower = index // 2, index % 2
+    return upper + lower * (size - 1 - 2 * upper)
+
+
+def index_of(place, size):
+    lower = place // (size // 2)
+    upper = place + lower * (size - 1 - 2 * place)
+    return upper * 2 + lower
+
+
+def greet(partners):
+    barrier = pltpu.get_barrier_semaphore()
+    for partner in partners:
+        pl.semaphore_signal(barrier, inc=1, device_id=partner, device_id_type=MESH)
+    pl.semaphore_wait(barrier, len(partners))
+
+
+def gather_kernel(size, x_ref, out_ref, send_sems, recv_sems):
+    row = lax.axis_index("row")
+    col = lax.axis_index("col")
+    place = place_of(row, size)
+    right = (index_of((place + 1) % size, size), col)
+    left = (index_of((place + size - 1) % size, size), col)
+    half = x_ref.shape[0] // 2
+    greet((left, right))
+    out_ref[row] = x_ref[...]
+    copies = []
+    for step in range(size - 1):
+        now = []
+        for way, (partner, owner) in enumerate(
+            ((right, place + size - step), (left, place + step))
+        ):
+            block = out_ref.at[index_of(owner % size, size), pl.ds(way * half, half)]
+            copy = pltpu.make_async_remote_copy(
+                src_ref=block,
+                dst_ref=block,
+                send_sem=send_sems.at[way, step],
+                recv_sem=recv_sems.at[way, step],
+                device_id=partner,
+                device_id_type=MESH,
+            )
+            copy.start()
+            now.append(copy)
+        for copy in now:
+            copy.wait_recv()
+        copies += now
+    for copy in copies:
+        copy.wait_send()
+
+
+def gather_rows(x):
+    size = lax.axis_size("row")
+    out = pl.pallas_call(
+        functools.partial(gather_kernel, size),
+        out_shape=jax.ShapeDtypeStruct((size, *x.shape), x.dtype),
+        in_specs=[pl.BlockSpec(memory_space=pltpu.VMEM)],
+        out_specs=pl.BlockSpec(memory_space=pltpu.VMEM),
+        scratch_shapes=[
+            pltpu.SemaphoreType.DMA((2, size - 1)),
+            pltpu.SemaphoreType.DMA((2, size - 1)),
+        ],
+        compiler_params=pltpu.CompilerParams(
+            collective_id=0, has_side_effects=True, vmem_limit_bytes=VMEM_LIMIT
+        ),
+    )(x)
+    return out.reshape(size * x.shape[0], x.shape[1])
+
+
+def partners_of(sizes):
+    here = [lax.axis_index("row"), lax.axis_index("col")]
+    found = []
+    for axis in (1, 0):
+        reach = 1
+        while reach < sizes[axis]:
+            bit = (here[axis] // reach) % 2
+            there = list(here)
+            there[axis] = here[axis] + (1 - 2 * bit) * reach
+            found.append((bit, tuple(there)))
+            reach *= 2
+    return found
+
+
+def sum_kernel(sizes, x_ref, out_ref, acc, landing, send_sems, recv_sems):
+    partners = partners_of(sizes)
+    greet([partner for _, partner in partners])
+    acc[...] = x_ref[...]
+    begin = 0
+    length = x_ref.shape[0]
+    offset = 0
+    begins = []
+    for stage, (bit, partner) in enumerate(partners):
+        length //= 2
+        keep = begin + bit * length
+        give = begin + (1 - bit) * length
+        copy = pltpu.make_async_remote_copy(
+            src_ref=acc.at[pl.ds(pl.multiple_of(give, 8), length)],
+            dst_ref=landing.at[pl.ds(offset, length)],
+            send_sem=send_sems.at[0, stage],
+            recv_sem=recv_sems.at[0, stage],
+            device_id=partner,
+            device_id_type=MESH,
+        )
+        copy.start()
+        copy.wait()
+        keep = pl.multiple_of(keep, 8)
+        acc[pl.ds(keep, length), :] += landing[offset : offset + length, :]
+        offset += length
+        begins.append(begin)
+        begin = keep
+    out_ref[pl.ds(begin, length), :] = acc[pl.ds(begin, length), :]
+    for stage in reversed(range(len(partners))):
+        block = out_ref.at[pl.ds(pl.multiple_of(begin, 8), length)]
+        copy = pltpu.make_async_remote_copy(
+            src_ref=block,
+            dst_ref=block,
+            send_sem=send_sems.at[1, stage],
+            recv_sem=recv_sems.at[1, stage],
+            device_id=partners[stage][1],
+            device_id_type=MESH,
+        )
+        copy.start()
+        copy.wait()
+        begin = begins[stage]
+        length *= 2
+
+
+def sum_all(x):
+    sizes = (lax.axis_size("row"), lax.axis_size("col"))
+    stages = sum(size.bit_length() - 1 for size in sizes)
+    return pl.pallas_call(
+        functools.partial(sum_kernel, sizes),
+        out_shape=jax.ShapeDtypeStruct(x.shape, x.dtype),
+        in_specs=[pl.BlockSpec(memory_space=pltpu.VMEM)],
+        out_specs=pl.BlockSpec(memory_space=pltpu.VMEM),
+        scratch_shapes=[
+            pltpu.VMEM(x.shape, x.dtype),
+            pltpu.VMEM(x.shape, x.dtype),
+            pltpu.SemaphoreType.DMA((2, stages)),
+            pltpu.SemaphoreType.DMA((2, stages)),
+        ],
+        compiler_params=pltpu.CompilerParams(
+            collective_id=1, has_side_effects=True, vmem_limit_bytes=VMEM_LIMIT
+        ),
+        cost_estimate=pl.CostEstimate(flops=0, bytes_accessed=200_000_000, transcendentals=0),
+    )(x)
 
 
 def values_index(step, rows_ref, cols_ref, count_ref):
@@ -168,7 +319,7 @@
     accounts = acc_feats.shape[0]
     chunks = lax.axis_size("col")
 
-    source = lax.all_gather(content_feats.T, "row", axis=0, tiled=True)
+    source = gather_rows(content_feats.T)
     partial = forward_tiles(vals, rows, cols, count, source, chunks)
     summed = lax.psum_scatter(partial, "col", scatter_dimension=0, tiled=True)[0]
     degree = summed[accounts].reshape(-1)[:accounts]
@@ -190,7 +341,7 @@
     norm_factor = 1.0 / math.sqrt(acc_total)
     both = jnp.concatenate([acc_feats, neigh], axis=1)
     weight_term = lax.dot_general(both, d_pre, (((0,), (0,)), ((), ())), precision=high)
-    weight_grads = lax.psum(weight_term * norm_factor, ("row", "col"))
+    weight_grads = sum_all(weight_term * norm_factor)
     features = acc_feats.shape[1]
     return (layer_out, grad_acc, grad_content, weight_grads[:features], weight_grads[features:])
 

time: 447 us -> 319 us (0.71)
  waiting for transfers between devices: 377 us -> 96.7 us
  Pallas kernels: 21.5 us -> 176 us
    pallas_call x0 -> x2, Pallas kernels: none -> 141 us  [the longest x1 89.7 us: sum_all(): pl.pallas_call(functools.partial(sum_kernel, sizes), out_shape=jax.ShapeD...]
    psum x1 -> x0, waiting for transfers between devices: 122 us -> none  [local(): weight_grads = lax.psum(weight_term * norm_factor, ('row', 'col'))]
    all_gather x1 -> x0, waiting for transfers between devices: 77.7 us -> none  [local(): source = lax.all_gather(content_feats.T, 'row', axis=0, tiled=True)]
    reduce_scatter x1, waiting for transfers between devices: 88 us -> 12 us  [local(): lax.psum_scatter(back_part, 'row', scatter_dimension=0, tiled=True)]
    reduce_scatter x1, waiting for transfers between devices: 59.8 us -> 50.3 us  [local(): lax.psum_scatter(partial, 'col', scatter_dimension=0, tiled=True)[0]]
    pallas_call x1, Pallas kernels: 11.1 us -> 17.7 us  [forward_tiles(): pl.pallas_call(functools.partial(forward_kernel, per_chunk), out_shape=ja...]
    pallas_call x1, Pallas kernels: 10.4 us -> 16.9 us  [backward_tiles(): pl.pallas_call(backward_kernel, out_shape=jax.ShapeDtypeStruct((channels,...]
    all_gather x1, waiting for transfers between devices: 28.3 us -> 34.4 us  [local(): grad_rows = lax.all_gather(d_gathered, 'col', axis=0, tiled=True)]
  transfers between devices with their start and end apart: 5 -> 3, of which waited for: 5 -> 3; matrix products, arithmetic and copies ran while one was open for 4% -> 5% of each run, Pallas kernels for 2% -> 28%
where the time goes in v2:
time: 319 us; the launch traced here: 315 us
  Pallas kernels  176 us (55%)
  waiting for transfers between devices  96.7 us (30%)
  matrix products  14.9 us (5%)
  between operations  14.6 us (5%)
  local copies, waits for them, and re-layouts  8.76 us (3%)
  other arithmetic  4.08 us (1%)
    pallas_call x1, Pallas kernels, sum_all(): pl.pallas_call(functools.partial(sum_kernel, sizes), out_shape=jax.ShapeD...  89.7 us
    pallas_call x1, Pallas kernels, gather_rows(): pl.pallas_call(functools.partial(gather_kernel, size), out_shape=jax.Shap...  51.7 us
    reduce_scatter x1, waiting for transfers between devices, local(): lax.psum_scatter(partial, 'col', scatter_dimension=0, tiled=True)[0]  50.3 us
    all_gather x1, waiting for transfers between devices, local(): grad_rows = lax.all_gather(d_gathered, 'col', axis=0, tiled=True)  34.4 us
    pallas_call x1, Pallas kernels, forward_tiles(): pl.pallas_call(functools.partial(forward_kernel, per_chunk), out_shape=ja...  17.7 us
    pallas_call x1, Pallas kernels, backward_tiles(): pl.pallas_call(backward_kernel, out_shape=jax.ShapeDtypeStruct((channels,...  16.9 us
    reduce_scatter x1, waiting for transfers between devices, local(): lax.psum_scatter(back_part, 'row', scatter_dimension=0, tiled=True)  12 us
    unnamed x22, local copies, waits for them, and re-layouts  7.28 us
  transfers between devices with their start and end apart: 3, of which 3 were waited for; matrix products, arithmetic and copies ran while one was open for 5% of the time, Pallas kernels for 28%

profile of v2, /device:TPU:0, one launch (start us, length us, event | category | flops | bytes accessed | tf_op | source)
XLA Modules:
  0.0 315.5 jit_solution(11286148909280447918)
XLA Ops:
  7.2 0.0 copy-start
  7.2 0.0 reduce-scatter.3.cloned.1.call-start
  8.0 0.0 copy-start.2
  8.0 1.0 copy-done.2
  9.0 0.0 copy-start.3
  9.0 0.0 copy-start.4
  9.0 51.7 %shard_map.128 = f32[8,64,2048]{2,1,0:T(8,128)S(1)} custom-call(f32[64,2048]{1,0:T(8,128)S(1)} %bitcast.24), custom_call_target="tpu_custom_call" | custom-call | tf_op jit(solution)/shard_map/pallas_call | solution.py:150
  60.7 0.0 copy-done.3
  60.7 0.0 copy-done.4
  60.8 17.7 %shard_map.129 = f32[4,520,512]{2,1,0:T(8,128)} custom-call(s32[128]{0:T(128)S(1)} %bitcast.25, s32[128]{0:T(128)S(1)} %bitcast.27, s32[1]{0:T(128)} %bitcast.21.count_ref, f32[128,128,128]{2,1,0:T(8,128)} %bitcast.29, f32[512,2048]{1,0:T(8,128)S(1)} %bitcast.23), custom_call_target="tpu_custom_call" | custom-call | flops 4294967296 | bytes 16000000 | tf_op jit(solution)/shard_map/pallas_call | solution.py:258
  78.4 0.0 reduce-scatter.3.cloned.1.call-update
  78.5 0.0 copy-start.5
  78.5 0.0 all-gather.2.cloned.1.call-start
  78.5 1.6 copy.15
  80.2 0.0 copy-done.5
  80.2 3.2 %fusion.12 = f32[512,512]{0,1:T(8,128)} fusion(f32[512,512]{1,0:T(8,128)S(1)} %copy-done.5, f32[512,512]{1,0:T(8,128)} %param.15), kind=kOutput, calls=%fused_computation.21 | convolution fusion | flops 805306368 | bytes 3145728 | tf_op jit(solution)/shard_map/dot_general | solution.py:328
  83.4 50.3 %reduce-scatter.3.cloned.1.call-done = f32[1,520,512]{2,1,0:T(8,128)} async-done(((f32[4,520,512]{2,1,0:T(8,128)}), f32[1,520,512]{2,1,0:T(8,128)}) %reduce-scatter.3.cloned.1.call-update) | async-done | bytes 1064976 | tf_op jit(solution)/shard_map/reduce_scatter | solution.py:324
  133.7 0.0 copy-start.9
  133.7 0.8 fusion.9
  134.5 1.4 fusion.7
  135.8 0.0 copy-done
  135.9 0.0 copy-done.9
  135.9 0.0 copy-start.8
  135.9 1.2 multiply_reduce_fusion.1
  137.1 0.0 copy-done.8
  137.2 0.4 multiply_reduce_fusion
  137.5 1.5 add_multiply_fusion
  139.1 2.8 convolution_multiply_fusion
  141.9 0.0 all-gather.2.cloned.1.call-update
  141.9 0.2 reduce-scatter.5.cloned.1.call-start
  142.1 34.4 %all-gather.2.cloned.1.call-done.grad_ref = f32[2048,512]{1,0:T(8,128)} async-done(((f32[512,512]{1,0:T(8,128)}), f32[2048,512]{1,0:T(8,128)}) %all-gather.2.cloned.1.call-update) | async-done | bytes 4194320 | tf_op jit(solution)/shard_map/all_gather | solution.py:336
  176.6 16.9 %shard_map.130 = f32[512,2048]{1,0:T(8,128)S(1)} custom-call(s32[128]{0:T(128)S(1)} %bitcast.26, s32[128]{0:T(128)S(1)} %bitcast.28, s32[1]{0:T(128)} %bitcast.22.count_ref, f32[128,128,128]{2,1,0:T(8,128)} %bitcast.30, f32[2048,512]{1,0:T(8,128)} %all-gather.2.cloned.1.call-done.grad_ref), custom_call_target="tpu_custom_call" | custom-call | flops 4294967296 | bytes 16000000 | tf_op jit(solution)/shard_map/pallas_call | solution.py:284
  193.5 0.0 copy-start.1
  193.5 1.9 copy-done.1
  195.5 0.0 reduce-scatter.5.cloned.1.call-update
  195.5 0.0 copy-start.6
  195.5 2.6 copy.16
  198.1 0.0 copy-done.6
  198.1 4.7 %fusion.4.x_ref = f32[1024,512]{1,0:T(8,128)S(1)} fusion(f32[512,512]{0,1:T(8,128)S(1)} %get-tuple-element.12, f32[512,512]{1,0:T(8,128)} %copy-done.8, f32[512,512]{1,0:T(8,128)S(1)} %copy-done.6), kind=kOutput, calls=%fused_computation.4 | convolution fusion | flops 1611661312 | bytes 5242880 | tf_op jit(solution)/shard_map/dot_general | solution.py:343
  202.9 0.0 copy-start.7
  202.9 89.7 %shard_map.131 = f32[1024,512]{1,0:T(8,128)S(1)} custom-call(f32[1024,512]{1,0:T(8,128)S(1)} %fusion.4.x_ref), custom_call_target="tpu_custom_call" | custom-call | bytes 200000000 | tf_op jit(solution)/shard_map/pallas_call | solution.py:227
  292.6 0.0 copy-done.7
  292.6 2.9 fusion.13
  295.5 1.5 fusion.11
  296.9 12.0 %reduce-scatter.5.cloned.1.call-done = f32[64,2048]{1,0:T(8,128)} async-done(((f32[512,2048]{1,0:T(8,128)}), f32[64,2048]{1,0:T(8,128)}) %reduce-scatter.5.cloned.1.call-update) | async-done | bytes 524304 | tf_op jit(solution)/shard_map/reduce_scatter | solution.py:338
  (2 shorter events, 0.0 us)
Async XLA Ops:
  7.2 128.7 %copy-start = (f32[512,512]{1,0:T(8,128)S(1)}, f32[512,512]{1,0:T(8,128)}, u32[]{:S(2)}) copy-start(f32[512,512]{1,0:T(8,128)} %param.16) | copy-start | bytes 3145732
  7.2 126.5 %reduce-scatter.3.cloned.1.call-start = ((), (), s32[]{:S(2)}) async-start(), calls=%async_computation.2 | async-start | bytes 5324800 | tf_op jit(solution)/shard_map/reduce_scatter | solution.py:324
  8.0 1.0 copy-start.2
  9.0 51.7 %copy-start.3 = (s32[1,1,128]{2,1,0:T(1,128)S(1)}, s32[1,1,128]{2,1,0:T(1,128)}, u32[]{:S(2)}) copy-start(s32[1,1,128]{2,1,0:T(1,128)} %param.12) | copy-start | bytes 1540
  9.0 51.7 %copy-start.4 = (s32[1,1,128]{2,1,0:T(1,128)S(1)}, s32[1,1,128]{2,1,0:T(1,128)}, u32[]{:S(2)}) copy-start(s32[1,1,128]{2,1,0:T(1,128)} %param.13) | copy-start | bytes 1540
  78.5 1.7 copy-start.5
  78.5 98.1 %all-gather.2.cloned.1.call-start = ((), (), s32[]{:S(2)}) async-start(), calls=%async_computation.3 | async-start | bytes 5242880 | tf_op jit(solution)/shard_map/all_gather | solution.py:336
  133.7 2.2 copy-start.9
  135.9 1.3 copy-start.8
  141.9 167.0 %reduce-scatter.5.cloned.1.call-start = ((), (), s32[]{:S(2)}) async-start(), calls=%async_computation.4 | async-start | bytes 4718592 | tf_op jit(solution)/shard_map/reduce_scatter | solution.py:338
  193.5 1.9 copy-start.1
  195.5 2.6 copy-start.6
  202.9 89.7 %copy-start.7 = (f32[512,512]{1,0:T(8,128)S(1)}, f32[512,512]{1,0:T(8,128)}, u32[]{:S(2)}) copy-start(f32[512,512]{1,0:T(8,128)} %param.15) | copy-start | bytes 3145732
Sparse Core Ops, SparseCore 0:
  78.6 55.0 reduce-scatter.2
  142.0 34.4 all-gather.1
  195.6 113.2 reduce-scatter.4

commit v3 on v2

--- a/solution.py
+++ b/solution.py
@@ -51,7 +51,7 @@
             product = jnp.dot(left, xs[col], preferred_element_type=jnp.float32)
             chunk = row // per_chunk
             begin = pl.multiple_of((row - chunk * per_chunk) * BLK, BLK)
-            out_ref[chunk, pl.ds(begin, BLK), :] += product[:BLK] + product[BLK:]
+            out_ref[reversed_bits(chunk, chunks), pl.ds(begin, BLK), :] += product[:BLK] + product[BLK:]
             degs[row] += lax.dot_general(
                 ones,
                 jnp.concatenate([hi, lo], axis=1),
@@ -63,7 +63,8 @@
     def _():
         for row in range(BR):
             chunk, place = row // per_chunk, row % per_chunk
-            out_ref[chunk, chunk_rows - PAD :, place * BLK : (place + 1) * BLK] = degs[row]
+            turned = reversed_bits(chunk, chunks)
+            out_ref[turned, chunk_rows - PAD :, place * BLK : (place + 1) * BLK] = degs[row]
 
 
 def backward_kernel(rows_ref, cols_ref, count_ref, vals_ref, grad_ref, out_ref, gs):
@@ -177,9 +178,100 @@
     return found
 
 
-def sum_kernel(sizes, x_ref, out_ref, acc, landing, send_sems, recv_sems):
+def scatter_kernel(size, x_ref, out_ref, acc, landing, send_sems, recv_sems):
+    stages = size.bit_length() - 1
+    partners = partners_of((1, size))
+    greet([partner for _, partner in partners])
+    begin = 0
+    length = size
+    offset = 0
+    for stage, (bit, partner) in enumerate(partners):
+        length //= 2
+        source = x_ref if stage == 0 else acc
+        keep = begin + bit * length
+        give = begin + (1 - bit) * length
+        copy = pltpu.make_async_remote_copy(
+            src_ref=source.at[pl.ds(give, length)],
+            dst_ref=landing.at[pl.ds(offset, length)],
+            send_sem=send_sems.at[stage],
+            recv_sem=recv_sems.at[stage],
+            device_id=partner,
+            device_id_type=MESH,
+        )
+        copy.start()
+        copy.wait()
+        total = source[pl.ds(keep, length)] + landing[offset : offset + length]
+        if stage == stages - 1:
+            out_ref[...] = total
+        else:
+            acc[pl.ds(keep, length)] = total
+        offset += length
+        begin = keep
+
+
+def scatter_cols(x):
+    size = x.shape[0]
+    stages = size.bit_length() - 1
+    return pl.pallas_call(
+        functools.partial(scatter_kernel, size),
+        out_shape=jax.ShapeDtypeStruct((1, *x.shape[1:]), x.dtype),
+        in_specs=[pl.BlockSpec(memory_space=pltpu.VMEM)],
+        out_specs=pl.BlockSpec(memory_space=pltpu.VMEM),
+        scratch_shapes=[
+            pltpu.VMEM(x.shape, x.dtype),
+            pltpu.VMEM(x.shape, x.dtype),
+            pltpu.SemaphoreType.DMA((stages,)),
+            pltpu.SemaphoreType.DMA((stages,)),
+        ],
+        compiler_params=pltpu.CompilerParams(
+            collective_id=2, has_side_effects=True, vmem_limit_bytes=VMEM_LIMIT
+        ),
+    )(x)
+
+
+def sum_kernel(
+    sizes, x_ref, parts_ref, out_ref, part_ref, acc, landing, slots, send_sems, recv_sems, ring_send, ring_recv
+):
+    size = sizes[0]
+    row = lax.axis_index("row")
+    col = lax.axis_index("col")
+    place = place_of(row, size)
+    right = (index_of((place + 1) % size, size), col)
+    left = (index_of((place + size - 1) % size, size), col)
+    half = part_ref.shape[0] // 2
     partners = partners_of(sizes)
-    greet([partner for _, partner in partners])
+    greet([partner for _, partner in partners] + [left, right])
+    ring = []
+
+    def ring_copy(step, way):
+        partner = (right, left)[way]
+        first = index_of((place + (size - 1, 1)[way]) % size, size)
+        source = parts_ref.at[first, pl.ds(way * half, half)] if step == 0 else slots.at[way, step - 1]
+        copy = pltpu.make_async_remote_copy(
+            src_ref=source,
+            dst_ref=slots.at[way, step],
+            send_sem=ring_send.at[way, step],
+            recv_sem=ring_recv.at[way, step],
+            device_id=partner,
+            device_id_type=MESH,
+        )
+        copy.start()
+        return copy
+
+    def ring_step():
+        step = len(ring) // 2 - 1
+        for way in range(2):
+            ring[2 * step + way].wait_recv()
+            owner = (place + (2 * size - 2 - step, 2 + step)[way]) % size
+            term = parts_ref[index_of(owner, size), pl.ds(way * half, half), :]
+            if step == size - 2:
+                part_ref[way * half : (way + 1) * half, :] = slots[way, step] + term
+            else:
+                slots[way, step] += term
+                ring.append(ring_copy(step + 1, way))
+
+    ring += [ring_copy(0, 0), ring_copy(0, 1)]
+    done = 0
     acc[...] = x_ref[...]
     begin = 0
     length = x_ref.shape[0]
@@ -198,6 +290,10 @@
             device_id_type=MESH,
         )
         copy.start()
+        for _ in range(2 if stage == 1 else 1):
+            if done < size - 1:
+                ring_step()
+                done += 1
         copy.wait()
         keep = pl.multiple_of(keep, 8)
         acc[pl.ds(keep, length), :] += landing[offset : offset + length, :]
@@ -216,30 +312,56 @@
             device_id_type=MESH,
         )
         copy.start()
+        if done < size - 1:
+            ring_step()
+            done += 1
         copy.wait()
         begin = begins[stage]
         length *= 2
-
-
-def sum_all(x):
+    while done < size - 1:
+        ring_step()
+        done += 1
+    for copy in ring:
+        copy.wait_send()
+
+
+def sum_all(x, parts):
     sizes = (lax.axis_size("row"), lax.axis_size("col"))
     stages = sum(size.bit_length() - 1 for size in sizes)
+    size = sizes[0]
+    channels, nodes = parts.shape
+    channels //= size
+    vmem = pl.BlockSpec(memory_space=pltpu.VMEM)
     return pl.pallas_call(
         functools.partial(sum_kernel, sizes),
-        out_shape=jax.ShapeDtypeStruct(x.shape, x.dtype),
-        in_specs=[pl.BlockSpec(memory_space=pltpu.VMEM)],
-        out_specs=pl.BlockSpec(memory_space=pltpu.VMEM),
+        out_shape=(
+            jax.ShapeDtypeStruct(x.shape, x.dtype),
+            jax.ShapeDtypeStruct((channels, nodes), x.dtype),
+        ),
+        in_specs=[vmem, vmem],
+        out_specs=(vmem, vmem),
         scratch_shapes=[
             pltpu.VMEM(x.shape, x.dtype),
             pltpu.VMEM(x.shape, x.dtype),
+            pltpu.VMEM((2, size - 1, channels // 2, nodes), x.dtype),
             pltpu.SemaphoreType.DMA((2, stages)),
             pltpu.SemaphoreType.DMA((2, stages)),
+            pltpu.SemaphoreType.DMA((2, size - 1)),
+            pltpu.SemaphoreType.DMA((2, size - 1)),
         ],
         compiler_params=pltpu.CompilerParams(
             collective_id=1, has_side_effects=True, vmem_limit_bytes=VMEM_LIMIT
         ),
-        cost_estimate=pl.CostEstimate(flops=0, bytes_accessed=200_000_000, transcendentals=0),
-    )(x)
+    )(x, parts.reshape(size, channels, nodes))
+
+
+def reversed_bits(index, size):
+    result = 0
+    while size > 1:
+        result = result * 2 + index % 2
+        index = index // 2
+        size //= 2
+    return result
 
 
 def values_index(step, rows_ref, cols_ref, count_ref):
@@ -321,7 +443,7 @@
 
     source = gather_rows(content_feats.T)
     partial = forward_tiles(vals, rows, cols, count, source, chunks)
-    summed = lax.psum_scatter(partial, "col", scatter_dimension=0, tiled=True)[0]
+    summed = scatter_cols(partial)[0]
     degree = summed[accounts].reshape(-1)[:accounts]
     inv_degree = lax.rsqrt(1.0 + degree)[:, None]
     neigh = summed[:accounts] * inv_degree
@@ -334,14 +456,15 @@
     d_pre = d_act * sigmoid_pre * (1.0 + pre_act * (1.0 - sigmoid_pre))
     d_gathered = jnp.dot(d_pre, w_neigh.T, precision=high) * inv_degree
     grad_rows = lax.all_gather(d_gathered, "col", axis=0, tiled=True)
-    back_part = backward_tiles(vals, rows, cols, count, grad_rows)
-    grad_content = lax.psum_scatter(back_part, "row", scatter_dimension=0, tiled=True).T
     grad_acc = jnp.dot(d_pre, w_self.T, precision=high)
     acc_total = accounts * lax.axis_size("row") * lax.axis_size("col")
     norm_factor = 1.0 / math.sqrt(acc_total)
     both = jnp.concatenate([acc_feats, neigh], axis=1)
-    weight_term = lax.dot_general(both, d_pre, (((0,), (0,)), ((), ())), precision=high)
-    weight_grads = sum_all(weight_term * norm_factor)
+    weight_term = lax.dot_general(both, d_pre, (((0,), (0,)), ((), ())), precision=high) * norm_factor
+    grad_rows, weight_term, grad_acc = lax.optimization_barrier((grad_rows, weight_term, grad_acc))
+    back_part = backward_tiles(vals, rows, cols, count, grad_rows)
+    weight_grads, grad_content = sum_all(weight_term, back_part)
+    grad_content = grad_content.T
     features = acc_feats.shape[1]
     return (layer_out, grad_acc, grad_content, weight_grads[:features], weight_grads[features:])
 

time: 319 us -> 291 us (0.912)
  waiting for transfers between devices: 96.7 us -> 20.7 us
  Pallas kernels: 176 us -> 224 us
  local copies, waits for them, and re-layouts: 8.76 us -> 12 us
    reduce_scatter x2 -> x0, waiting for transfers between devices: 62.3 us -> none  [the longest x1 50.3 us: local(): lax.psum_scatter(partial, 'col', scatter_dimension=0, tiled=True)[0]]
    pallas_call x1 -> x2, Pallas kernels: 89.7 us -> 140 us  [the longest x1 95.9 us: sum_all(): pl.pallas_call(functools.partial(sum_kernel, sizes), out_shape=(jax.Shape...]
    all_gather x1, waiting for transfers between devices: 34.4 us -> 20.7 us  [local(): grad_rows = lax.all_gather(d_gathered, 'col', axis=0, tiled=True)]
    unnamed x22 -> x29, local copies, waits for them, and re-layouts: 7.28 us -> 10.5 us
  transfers between devices with their start and end apart: 3 -> 1, of which waited for: 3 -> 1; matrix products, arithmetic and copies ran while one was open for 5% -> 4% of each run, Pallas kernels for 28% -> 0%
where the time goes in v3:
time: 291 us; the launch traced here: 286 us
  Pallas kernels  224 us (77%)
  waiting for transfers between devices  20.7 us (7%)
  between operations  15 us (5%)
  matrix products  12.9 us (4%)
  local copies, waits for them, and re-layouts  12 us (4%)
    pallas_call x1, Pallas kernels, sum_all(): pl.pallas_call(functools.partial(sum_kernel, sizes), out_shape=(jax.Shape...  95.9 us
    pallas_call x1, Pallas kernels, gather_rows(): pl.pallas_call(functools.partial(gather_kernel, size), out_shape=jax.Shap...  51.8 us
    pallas_call x1, Pallas kernels, scatter_cols(): pl.pallas_call(functools.partial(scatter_kernel, size), out_shape=jax.Sha...  44 us
    all_gather x1, waiting for transfers between devices, local(): grad_rows = lax.all_gather(d_gathered, 'col', axis=0, tiled=True)  20.7 us
    pallas_call x1, Pallas kernels, forward_tiles(): pl.pallas_call(functools.partial(forward_kernel, per_chunk), out_shape=ja...  16.3 us
    pallas_call x1, Pallas kernels, backward_tiles(): pl.pallas_call(backward_kernel, out_shape=jax.ShapeDtypeStruct((channels,...  15.8 us
    unnamed x29, local copies, waits for them, and re-layouts  10.5 us
  transfers between devices with their start and end apart: 1, of which 1 were waited for; matrix products, arithmetic and copies ran while one was open for 4% of the time, Pallas kernels for 0%

profile of v3, /device:TPU:0, one launch (start us, length us, event | category | flops | bytes accessed | tf_op | source)
XLA Modules:
  0.0 286.5 jit_solution(3584895876369182673)
XLA Ops:
  7.2 0.0 copy-start
  7.2 0.0 copy-start.3
  7.2 0.0 all-gather.2.cloned.1.call-start
  8.0 1.6 copy.15
  9.6 0.0 copy-done.3
  9.6 0.0 copy-start.4
  9.6 0.0 copy-start.5
  9.6 51.8 %shard_map.128 = f32[8,64,2048]{2,1,0:T(8,128)S(1)} custom-call(f32[64,2048]{1,0:T(8,128)S(1)} %bitcast.24), custom_call_target="tpu_custom_call" | custom-call | tf_op jit(solution)/shard_map/pallas_call | solution.py:151
  61.4 0.0 copy-done.4
  61.4 0.0 copy-done.5
  61.4 16.3 %shard_map.129.x_ref = f32[4,520,512]{2,1,0:T(8,128)} custom-call(s32[128]{0:T(128)S(1)} %bitcast.26, s32[128]{0:T(128)S(1)} %bitcast.28, s32[1]{0:T(128)} %bitcast.20.count_ref, f32[128,128,128]{2,1,0:T(8,128)} %bitcast.30, f32[512,2048]{1,0:T(8,128)S(1)} %bitcast.23), custom_call_target="tpu_custom_call" | custom-call | flops 4294967296 | bytes 16000000 | tf_op jit(solution)/shard_map/pallas_call | solution.py:380
  77.7 0.0 copy-start.1
  77.7 2.2 copy-done.1
  79.9 44.0 %shard_map.130 = f32[1,520,512]{2,1,0:T(8,128)S(1)} custom-call(f32[4,520,512]{2,1,0:T(8,128)S(1)} %copy-done.1), custom_call_target="tpu_custom_call" | custom-call | tf_op jit(solution)/shard_map/pallas_call | solution.py:215
  123.9 0.0 copy-start.7
  123.9 0.0 copy-start.9
  124.0 0.1 bitcast_multiply_fusion
  124.1 1.0 copy-done.7
  125.1 0.3 copy-done.9
  125.5 0.0 copy-start.11
  125.5 1.0 fusion.10
  126.5 0.0 copy-done
  126.5 1.3 multiply_reduce_fusion.1
  127.8 0.0 copy-done.11
  127.8 0.4 multiply_reduce_fusion
  128.2 1.5 add_multiply_fusion
  129.7 0.0 copy-start.6
  129.7 2.9 convolution_multiply_fusion
  132.6 0.0 copy-start.8
  132.6 0.0 all-gather.2.cloned.1.call-update
  132.6 2.6 copy.16
  135.2 0.0 copy-done.6
  135.2 0.0 copy-done.8
  135.2 0.0 copy-start.10
  135.2 0.0 copy-start.12
  135.2 2.9 %fusion.11 = f32[512,512]{1,0:T(8,128)} fusion(f32[512,512]{0,1:T(8,128)S(1)} %get-tuple-element.22, f32[512,512]{1,0:T(8,128)S(1)} %copy-done.8), kind=kOutput, calls=%fused_computation.20 | convolution fusion | flops 805306368 | bytes 3145728 | tf_op jit(solution)/shard_map/dot_general | solution.py:459
  138.1 0.0 copy-done.10
  138.1 0.0 copy-done.12
  138.1 4.8 %fusion.4.x_ref = f32[1024,512]{1,0:T(8,128)S(1)} fusion(f32[512,512]{0,1:T(8,128)} %copy-done.6, f32[512,512]{1,0:T(8,128)S(1)} %copy-done.12, f32[512,512]{1,0:T(8,128)S(1)} %copy-done.10), kind=kOutput, calls=%fused_computation.4 | convolution fusion | flops 1611661312 | bytes 5242880 | tf_op jit(solution)/shard_map/dot_general | solution.py:463
  143.0 20.7 %all-gather.2.cloned.1.call-done.grad_ref = f32[2048,512]{1,0:T(8,128)} async-done(((f32[512,512]{1,0:T(8,128)}), f32[2048,512]{1,0:T(8,128)}) %all-gather.2.cloned.1.call-update) | async-done | bytes 4194320 | tf_op jit(solution)/shard_map/all_gather | solution.py:458
  163.7 15.8 %shard_map.131 = f32[512,2048]{1,0:T(8,128)S(1)} custom-call(s32[128]{0:T(128)S(1)} %bitcast.27, s32[128]{0:T(128)S(1)} %bitcast.29, s32[1]{0:T(128)} %bitcast.21.count_ref, f32[128,128,128]{2,1,0:T(8,128)} %bitcast.31, f32[2048,512]{1,0:T(8,128)} %all-gather.2.cloned.1.call-done.grad_ref), custom_call_target="tpu_custom_call" | custom-call | flops 4294967296 | bytes 16000000 | tf_op jit(solution)/shard_map/pallas_call | solution.py:406
  179.5 0.0 copy-start.2
  179.5 1.9 copy-done.2
  181.4 95.9 %shard_map.132 = (f32[1024,512]{1,0:T(8,128)S(1)}, f32[64,2048]{1,0:T(8,128)S(1)}) custom-call(f32[1024,512]{1,0:T(8,128)S(1)} %fusion.4.x_ref, f32[8,64,2048]{2,1,0:T(8,128)} %bitcast.22), custom_call_target="tpu_custom_call" | custom-call | tf_op jit(solution)/shard_map/pallas_call | solution.py:335
  277.3 1.5 fusion.9
  278.8 0.8 copy.19
  (3 shorter events, 0.0 us)
Async XLA Ops:
  7.2 119.3 %copy-start = (f32[512,512]{1,0:T(8,128)S(1)}, f32[512,512]{1,0:T(8,128)}, u32[]{:S(2)}) copy-start(f32[512,512]{1,0:T(8,128)} %param.16) | copy-start | bytes 3145732
  7.2 2.4 copy-start.3
  7.2 156.5 %all-gather.2.cloned.1.call-start = ((), (), s32[]{:S(2)}) async-start(), calls=%async_computation | async-start | bytes 5242880 | tf_op jit(solution)/shard_map/all_gather | solution.py:458
  9.6 51.8 %copy-start.4 = (s32[1,1,128]{2,1,0:T(1,128)S(1)}, s32[1,1,128]{2,1,0:T(1,128)}, u32[]{:S(2)}) copy-start(s32[1,1,128]{2,1,0:T(1,128)} %param.12) | copy-start | bytes 1540
  9.6 51.8 %copy-start.5 = (s32[1,1,128]{2,1,0:T(1,128)S(1)}, s32[1,1,128]{2,1,0:T(1,128)}, u32[]{:S(2)}) copy-start(s32[1,1,128]{2,1,0:T(1,128)} %param.13) | copy-start | bytes 1540
  77.7 2.2 copy-start.1
  123.9 1.2 copy-start.7
  123.9 1.5 copy-start.9
  125.5 2.3 copy-start.11
  129.7 5.5 %copy-start.6 = (f32[512,512]{0,1:T(8,128)}, f32[512,512]{0,1:T(8,128)S(1)}, u32[]{:S(2)}) copy-start(f32[512,512]{0,1:T(8,128)S(1)} %get-tuple-element.22) | copy-start | bytes 3145732
  132.6 2.6 copy-start.8
  135.2 2.9 %copy-start.10 = (f32[512,512]{1,0:T(8,128)S(1)}, f32[512,512]{1,0:T(8,128)}, u32[]{:S(2)}) copy-start(f32[512,512]{1,0:T(8,128)} %param.9) | copy-start | bytes 3145732
  135.2 2.9 %copy-start.12 = (f32[512,512]{1,0:T(8,128)S(1)}, f32[512,512]{1,0:T(8,128)}, u32[]{:S(2)}) copy-start(f32[512,512]{1,0:T(8,128)} %copy-done.11) | copy-start | bytes 3145732
  179.5 1.9 copy-start.2
Sparse Core Ops, SparseCore 0:
  132.7 30.8 all-gather.1
